TPU v7x, 128 devices: a whole 4x4x4 slice. The times are simulated.
128 devices in a mesh: gx: 8 (over z, y_hi), gy: 4 (over x), gz: 4 (over y_lo, core).
Axes of the slice: x: 4, y: 4 (y_hi: 2, y_lo: 2; y = y_hi * 2 + y_lo), z: 4, core: 2. Of those that a mesh axis runs over, the one named last changes fastest.
Arguments:
- coarse_in: bfloat16 [32, 32, 2048], P('gx', 'gy', 'gz'), may hold values from -6 to 6
- out_grad: bfloat16 [64, 64, 4096], P('gx', 'gy', 'gz'), may hold values from -6 to 6
- up_weight: bfloat16 [64, 64, 64], replicated, may hold values from -0.25 to 0.25
- conv_weight: bfloat16 [27, 64, 64], replicated, may hold values from -0.15625 to 0.15625
Outputs:
- grad_coarse: bfloat16 [32, 32, 2048], P('gx', 'gy', 'gz')
- grad_up: float32 [64, 64, 64], replicated
- grad_conv: float32 [27, 64, 64], replicated
All inputs are finite; a program needn't handle non-finite values.
Results may differ from a plain program's by a relative error of at most 0.005.
Values may be sent and summed in bfloat16 or wider, within the bound.
A program may use at most 64 MiB of HBM per device.

v0:
```python
import functools
import itertools
import math

import jax
import jax.numpy as jnp
from jax import lax
from jax.experimental import pallas as pl
from jax.experimental.pallas import tpu as pltpu
from jax.sharding import PartitionSpec as P

MESH = pl.DeviceIdType.MESH
F32 = jnp.float32
BF16 = jnp.bfloat16
C = 64
gelu_coef = 0.7978845608
gelu_cube = 0.044715
taps_by_parity = (((0, 3), (1, 1)), ((1, 2), (2, 0)))
NEIGHBOURS = [o for o in itertools.product((-1, 0, 1), repeat=3) if any(o)]


def nt(left, right):
    return lax.dot_general(left, right, (((1,), (1,)), ((), ())), preferred_element_type=F32)


def nn(left, right):
    return jnp.dot(left, right, preferred_element_type=F32)


class Place:
    def __init__(self, sizes):
        self.sizes = sizes
        self.gx, self.gy, self.gz = (lax.axis_index(a) for a in ("gx", "gy", "gz"))
        self.nz, self.nx, self.ny = sizes[0] // 2, sizes[1], sizes[2]
        self.low = sizes[2] // 2
        self.z, self.x = self.gx // 2, self.gy
        self.y = self.gx % 2 * self.low + self.gz // 2
        self.core = self.gz % 2
        self.index = self.z * self.nx + self.x
        self.group = self.nz * self.nx
        self.row_group = 2 * self.low

    def neighbour(self, o):
        me = (self.gx, self.gy, self.gz)
        return tuple(lax.rem(m + d + n, n) for m, d, n in zip(me, o, self.sizes))

    def sibling(self):
        return (self.gx, self.gy, self.gz + 1 - 2 * self.core)

    def in_group(self, dz, dx):
        z, x = lax.rem(self.z + dz, self.nz), lax.rem(self.x + dx, self.nx)
        return (z * 2 + self.gx % 2, x, self.gz), z * self.nx + x

    def in_row(self, dy):
        y = lax.rem(self.y + dy, self.row_group)
        return (self.z * 2 + y // self.low, self.x, y % self.low * 2 + self.core)

    def group_steps(self):
        return [o for o in itertools.product(range(self.nz), range(self.nx)) if any(o)]


def remote(src, dst, send, recv, device):
    return pltpu.make_async_remote_copy(
        src_ref=src, dst_ref=dst, send_sem=send, recv_sem=recv, device_id=device, device_id_type=MESH
    )


def fine_halo(place, xt, ys, yt, send, recv):
    copies = []
    nx, lanes = xt.shape[0] - 2, xt.shape[2] - 256
    for i, (ox, oy, oz) in enumerate(NEIGHBOURS):
        zs, zd = {
            0: (pl.ds(0, lanes), pl.ds(128, lanes)),
            1: (pl.ds(lanes - 128, 128), pl.ds(0, 128)),
            -1: (pl.ds(0, 128), pl.ds(lanes + 128, 128)),
        }[oz]
        if oy == 0:
            zs = pl.ds(zs.start + 128, zs.size)
            xs, xd = {0: (pl.ds(1, nx), pl.ds(1, nx)), 1: (nx, 0), -1: (1, nx + 1)}[ox]
            src, dst = xt.at[xs, :, zs], xt.at[xd, :, zd]
        else:
            side = (1 - oy) // 2
            src, dst = ys.at[side, :, zs], yt.at[side, 1 - ox, :, zd]
        copies.append(remote(src, dst, send.at[i], recv.at[i], place.neighbour((ox, oy, oz))))
    for copy in copies:
        copy.start()
    return copies


def coarse_halo(place, ue, us, yt, send, recv):
    copies = []
    nx, lanes = ue.shape[0] - 2, ue.shape[2] - 256
    for i, (ox, oy, oz) in enumerate(NEIGHBOURS):
        zs, zd = {
            0: (pl.ds(0, lanes), pl.ds(128, lanes)),
            1: (pl.ds(lanes - 128, 128), pl.ds(0, 128)),
            -1: (pl.ds(0, 128), pl.ds(lanes + 128, 128)),
        }[oz]
        if oy == 0:
            zs = pl.ds(zs.start + 128, zs.size)
            xs, xd = {0: (pl.ds(1, nx), pl.ds(1, nx)), 1: (nx, 0), -1: (1, nx + 1)}[ox]
            src, dst = ue.at[xs, pl.ds(8, 8), zs], ue.at[xd, pl.ds(8, 8), zd]
        else:
            side = (1 - oy) // 2
            src, dst = us.at[side, :, zs], yt.at[side, 1 - ox, :, zd]
        copies.append(remote(src, dst, send.at[i], recv.at[i], place.neighbour((ox, oy, oz))))
    for copy in copies:
        copy.start()
    return copies


def fill_fine(xt, yt, yr, ge):
    nx, pairs = xt.shape[0] - 2, ge.shape[0]
    wide = 128 * pairs
    turn = xt.shape[2] - 64
    for side in range(2):
        for slot in range(3):
            yr[side, slot] = pltpu.roll(yt[side, slot], turn, 1)[:, :wide]
    for x in range(nx + 2):
        turned = pltpu.roll(xt[x].astype(F32), turn, 1)
        slot, row = (0, nx - 1) if x == 0 else (2, 0) if x == nx + 1 else (1, x - 1)
        for pair in range(pairs):
            lanes = slice(128 * pair, 128 * pair + 128)
            ge[pair, x, 8:24, :] = turned[:, lanes]
            ge[pair, x, 7:8, :] = yr[0, slot, row : row + 1, lanes]
            ge[pair, x, 24:25, :] = yr[1, slot, row : row + 1, lanes]


class AllReduce:
    def __init__(self, place, total, fin, r1, s, r2, r3, sems):
        self.place, self.total, self.fin = place, total, fin
        self.r1, self.s, self.r2, self.r3, self.sems = r1, s, r2, r3, sems
        self.half = total.shape[0] // 2
        self.piece = self.half // place.group
        self.used = 0
        self.flight = []

    def send(self, src, dst, device):
        i = self.used
        self.used += 1
        copy = remote(src, dst, self.sems.at[0, i], self.sems.at[1, i], device)
        copy.start()
        self.flight.append(copy)

    def arrive(self):
        for copy in self.flight:
            copy.wait()
        self.flight = []

    def mine(self, index, size):
        return pl.ds(pl.multiple_of(index * size, size), size)

    def pair(self):
        p = self.place
        self.send(self.total.at[self.mine(1 - p.core, self.half)], self.r1, p.sibling())

    def scatter(self):
        p = self.place
        self.arrive()
        self.s[...] = (self.total[self.mine(p.core, self.half), :] + self.r1[...]).astype(BF16)
        for k, o in enumerate(p.group_steps()):
            device, index = p.in_group(*o)
            self.send(self.s.at[self.mine(index, self.piece)], self.r2.at[k], device)

    def exchange(self):
        p = self.place
        self.arrive()
        total = self.s[self.mine(p.index, self.piece), :].astype(F32)
        for k in range(p.group - 1):
            total = total + self.r2[k].astype(F32)
        self.r3[p.y] = total.astype(BF16)
        for dy in range(1, p.row_group):
            self.send(self.r3.at[p.y], self.r3.at[p.y], p.in_row(dy))

    def spot(self):
        p = self.place
        return pl.ds(pl.multiple_of(p.core * self.half + p.index * self.piece, self.piece), self.piece)

    def gather(self):
        p = self.place
        self.arrive()
        total = self.r3[0].astype(F32)
        for k in range(1, p.row_group):
            total = total + self.r3[k].astype(F32)
        self.fin[self.spot(), :] = total.astype(BF16)
        for o in p.group_steps():
            device, _ = p.in_group(*o)
            self.send(self.fin.at[self.spot()], self.fin.at[self.spot()], device)

    def share(self):
        p = self.place
        self.arrive()
        spot = self.mine(p.core, self.half)
        self.send(self.fin.at[spot], self.fin.at[spot], p.sibling())


def main_kernel(
    sizes, u_in, g_in, wu_in, wc_in,
    coarse_out, fin_up, fin_conv,
    ub, wu, wc, ue, ue1, us, uyt, gxt, gf, ys, gyt, gyr, ge, gd,
    wp, cw, w3, uw, uwt, pre, slope, ht, gh, gp, pxt, pys, pyt, gc,
    a_up, a_conv, up_r1, up_s, up_r2, up_r3, cv_r1, cv_s, cv_r2, cv_r3,
    local_sems, u_sems, g_sems, p_sems, up_sems, cv_sems,
):
    place = Place(sizes)
    barrier = pltpu.get_barrier_semaphore()
    partners = [place.neighbour(o) for o in NEIGHBOURS]
    partners += [place.in_group(*o)[0] for o in place.group_steps()]
    partners += [place.in_row(dy) for dy in range(1, place.row_group)]
    partners += [place.sibling()]
    for device in partners:
        pl.semaphore_signal(barrier, inc=1, device_id=device, device_id_type=MESH)
    loads = [
        pltpu.make_async_copy(u_in, ub, local_sems.at[0]),
        pltpu.make_async_copy(g_in, gxt.at[pl.ds(1, 8), :, pl.ds(128, 1024)], local_sems.at[1]),
        pltpu.make_async_copy(wu_in, wu, local_sems.at[2]),
        pltpu.make_async_copy(wc_in, wc, local_sems.at[3]),
    ]
    for load in loads:
        load.start()

    loads[0].wait()
    for x in range(4):
        ue[1 + x, 8:16, 128:640] = ub[x].astype(F32)
    for x in range(4):
        us[0, x : x + 1, :] = ue[1 + x, 15:16, 128:640]
        us[1, x : x + 1, :] = ue[1 + x, 8:9, 128:640]
    us[0, 4:8, :] = jnp.zeros((4, 512), F32)
    us[1, 4:8, :] = jnp.zeros((4, 512), F32)
    loads[1].wait()
    for x in range(8):
        gf[x] = gxt[1 + x, :, 128:1152].astype(F32)
    for x in range(8):
        ys[0, x : x + 1, :] = gf[x, 15:16, :]
        ys[1, x : x + 1, :] = gf[x, 0:1, :]
    pl.semaphore_wait(barrier, len(partners))
    u_copies = coarse_halo(place, ue, us, uyt, u_sems.at[0], u_sems.at[1])
    g_copies = fine_halo(place, gxt, ys, gyt, g_sems.at[0], g_sems.at[1])

    loads[2].wait()
    loads[3].wait()
    blank = jnp.zeros((C, C), BF16)
    for q in range(16):
        k0, k1, k2, k3 = (wu[4 * q + k] for k in range(4))
        wp[q, 0:64, :] = jnp.concatenate([k3, blank], axis=1)
        wp[q, 64:128, :] = jnp.concatenate([k1, k2], axis=1)
        wp[q, 128:192, :] = jnp.concatenate([blank, k0], axis=1)
        wp[q, 192:256, :] = jnp.zeros((C, 2 * C), BF16)
        w3[q, :, 0:128] = jnp.concatenate([k0, k1], axis=1)
        w3[q, :, 128:256] = jnp.concatenate([k2, k3], axis=1)
    for t in range(9):
        d0, d1, d2 = (wc[3 * t + d] for d in range(3))
        cw[t, 0:64, 0:128] = jnp.concatenate([d2, d1], axis=1)
        cw[t, 0:64, 128:256] = jnp.concatenate([d0, blank], axis=1)
        cw[t, 64:128, 0:128] = jnp.concatenate([blank, d2], axis=1)
        cw[t, 64:128, 128:256] = jnp.concatenate([d1, d0], axis=1)

    for copy in u_copies:
        copy.wait()
    for x in range(6):
        slot, row = (0, 3) if x == 0 else (2, 0) if x == 5 else (1, x - 1)
        ue[x, 7:8, :] = uyt[0, slot, row : row + 1, :]
        ue[x, 16:17, :] = uyt[1, slot, row : row + 1, :]
    for x in range(6):
        ue1[x] = pltpu.roll(ue[x], 768 - 64, 1)[:, :640]
    for sx in range(3):
        for sy in range(3):
            rows = []
            for zc in range(8):
                if zc % 2:
                    part = ue[sx : sx + 4, 7 + sy : 15 + sy, 64 * (zc + 1) : 64 * (zc + 1) + 256]
                else:
                    part = ue1[sx : sx + 4, 7 + sy : 15 + sy, 64 * zc : 64 * zc + 256]
                rows.append(part.reshape(32, 256))
            window = jnp.concatenate(rows, axis=0)
            uw[3 * sx + sy] = window.astype(BF16)
            uwt[3 * sx + sy] = window.T.astype(BF16)[:192]

    for px in range(2):
        for py in range(2):
            total = None
            for sx, kx in taps_by_parity[px]:
                for sy, ky in taps_by_parity[py]:
                    part = nn(uw[3 * sx + sy], wp[4 * kx + ky])
                    total = part if total is None else total + part
            total = total.reshape(8, 4, 8, 128)
            for zc in range(8):
                for xc in range(4):
                    pre[zc, 2 * xc + px, pl.ds(py, 8, stride=2), :] = total[zc, xc]
    for zc in range(8):
        v = pre[zc].reshape(128, 128)
        square = v * v
        tangent = jnp.tanh(gelu_coef * (v + gelu_cube * (square * v)))
        hidden = 0.5 * v * (1.0 + tangent)
        ht[:, 128 * zc : 128 * zc + 128] = hidden.T.astype(BF16)
        slope[zc] = 0.5 * (1.0 + tangent) + 0.5 * v * (1.0 - tangent * tangent) * gelu_coef * (
            1.0 + 3.0 * gelu_cube * square
        )

    for copy in g_copies:
        copy.wait()
    fill_fine(gxt, gyt, gyr, ge)
    for x in range(10):
        for k in range(3):
            for pair in range(9):
                gd[k, x, :, 128 * pair : 128 * pair + 128] = ge[pair, x, 7 + k : 23 + k, :].astype(BF16)

    def windows(t):
        dx, dy = t // 3, t % 3
        parts = [
            gd[2 - dy, pl.ds(2 - dx, 8), :, 128 * zc : 128 * zc + 256].reshape(128, 256) for zc in range(8)
        ]
        return jnp.concatenate(parts, axis=0)

    gh[...] = jnp.zeros_like(gh)

    def hidden_step(t, carry):
        gh[...] += nt(windows(t), cw[t])
        return carry

    lax.fori_loop(0, 9, hidden_step, 0)
    for zc in range(8):
        grad = (gh[128 * zc : 128 * zc + 128, :] * slope[zc]).astype(BF16).reshape(8, 16, 128)
        pxt[1:9, :, 128 * zc + 128 : 128 * zc + 256] = grad
        gp[zc] = grad.astype(F32)
        for x in range(8):
            pys[0, x : x + 1, 128 * zc : 128 * zc + 128] = gp[zc, x, 15:16, :]
            pys[1, x : x + 1, 128 * zc : 128 * zc + 128] = gp[zc, x, 0:1, :]
    p_copies = fine_halo(place, pxt, pys, pyt, p_sems.at[0], p_sems.at[1])

    low = lax.broadcasted_iota(jnp.int32, (C, 2 * C), 1) < C
    for px in range(2):
        for py in range(2):
            rows = []
            for zc in range(8):
                for xc in range(4):
                    rows.append(gp[zc, 2 * xc + px, pl.ds(py, 8, stride=2), :])
            grad = jnp.concatenate(rows, axis=0).astype(BF16)
            for sx, kx in taps_by_parity[px]:
                for sy, ky in taps_by_parity[py]:
                    q = 4 * kx + ky
                    part = nn(uwt[3 * sx + sy], grad)
                    a_up[128 * q : 128 * q + 64, :] = part[64:128]
                    a_up[128 * q + 64 : 128 * q + 128, :] = jnp.where(low, part[0:64], part[128:192])
    up = AllReduce(place, a_up, fin_up, up_r1, up_s, up_r2, up_r3, up_sems)
    up.pair()

    def conv_step(t, carry):
        part = nn(ht[...], windows(t))
        gc[t] = part[:64] + pltpu.roll(part[64:], 256 - 64, 1)
        return carry

    lax.fori_loop(0, 4, conv_step, 0)
    up.scatter()
    lax.fori_loop(4, 9, conv_step, 0)
    for t in range(9):
        a_conv[64 * t : 64 * t + 64, :] = gc[t, :, 0:128]
    for m in range(5):
        if m < 4:
            other = pltpu.roll(gc[2 * m + 1, :, 128:256], 64, 1)
            joined = jnp.where(low, gc[2 * m, :, 128:256], other)
        else:
            joined = gc[8, :, 128:256]
        a_conv[64 * (9 + m) : 64 * (10 + m), :] = joined
    a_conv[896:1024, :] = jnp.zeros((128, 128), F32)
    conv = AllReduce(place, a_conv, fin_conv, cv_r1, cv_s, cv_r2, cv_r3, cv_sems)
    conv.pair()
    conv.scatter()
    up.exchange()

    for copy in p_copies:
        copy.wait()
    fill_fine(pxt, pyt, gyr, ge)
    total = None
    for kx in range(4):
        for ky in range(4):
            rows = []
            for zc in range(8):
                for xc in range(4):
                    rows.append(
                        jnp.concatenate(
                            [
                                ge[zc + s, 2 * xc + kx, pl.ds(7 + ky, 8, stride=2), :]
                                for s in range(2)
                            ],
                            axis=1,
                        )
                    )
            part = nt(jnp.concatenate(rows, axis=0).astype(BF16), w3[4 * kx + ky])
            total = part if total is None else total + part
        if kx == 1:
            up.gather()
            conv.exchange()
    total = total.reshape(8, 4, 8, C)
    for zc in range(0, 8, 2):
        coarse_out[:, :, 64 * zc : 64 * zc + 128] = jnp.concatenate(
            [total[zc], total[zc + 1]], axis=2
        ).astype(BF16)
    conv.gather()
    up.share()
    conv.share()
    up.arrive()
    conv.arrive()


def last_kernel(factor, coarse, fin_up, fin_conv, coarse_out, up_out, conv_out):
    coarse_out[...] = coarse[...]
    for q in range(16):
        first = fin_up[128 * q : 128 * q + 64, :].astype(F32) * factor
        second = fin_up[128 * q + 64 : 128 * q + 128, :].astype(F32) * factor
        up_out[4 * q + 1] = first[:, :C]
        up_out[4 * q + 2] = first[:, C:]
        up_out[4 * q + 3] = second[:, :C]
        up_out[4 * q] = second[:, C:]
    for t in range(9):
        both = fin_conv[64 * t : 64 * t + 64, :].astype(F32) * factor
        conv_out[3 * t + 2] = both[:, :C]
        conv_out[3 * t + 1] = both[:, C:]
        m = t // 2
        rest = fin_conv[64 * (9 + m) : 64 * (10 + m), :].astype(F32) * factor
        conv_out[3 * t] = rest[:, C:] if t % 2 else rest[:, :C]


def local(sizes, coarse_in, out_grad, up_weight, conv_weight):
    every_cell = 2048 * sizes[0] * sizes[1] * sizes[2]
    group = sizes[0] // 2 * sizes[1]
    row_group = sizes[2] // 2 * 2
    up_piece, cv_piece = 1024 // group, 512 // group
    messages = 2 + 2 * (group - 1) + row_group - 1
    vmem = pltpu.VMEM
    dma = pltpu.SemaphoreType.DMA
    whole = pl.BlockSpec(memory_space=vmem)
    anywhere = pl.BlockSpec(memory_space=pl.ANY)
    scratch = [
        vmem((4, 8, 512), BF16), vmem((64, C, C), BF16), vmem((27, C, C), BF16),
        vmem((6, 24, 768), F32), vmem((6, 24, 640), F32), vmem((2, 8, 512), F32), vmem((2, 3, 8, 768), F32),
        vmem((10, 16, 1280), BF16), vmem((8, 16, 1024), F32), vmem((2, 8, 1024), F32),
        vmem((2, 3, 8, 1280), F32), vmem((2, 3, 8, 1152), F32), vmem((9, 10, 32, 128), F32),
        vmem((3, 10, 16, 1152), BF16),
        vmem((16, 256, 128), BF16), vmem((9, 128, 256), BF16), vmem((16, 64, 256), BF16),
        vmem((9, 256, 256), BF16), vmem((9, 192, 256), BF16),
        vmem((8, 8, 16, 128), F32), vmem((8, 128, 128), F32), vmem((128, 1024), BF16), vmem((1024, 128), F32),
        vmem((8, 8, 16, 128), F32),
        vmem((10, 16, 1280), BF16), vmem((2, 8, 1024), F32), vmem((2, 3, 8, 1280), F32), vmem((9, 64, 256), F32),
        vmem((2048, 128), F32), vmem((1024, 128), F32),
        vmem((1024, 128), F32), vmem((1024, 128), BF16), vmem((group - 1, up_piece, 128), BF16),
        vmem((row_group, up_piece, 128), BF16),
        vmem((512, 128), F32), vmem((512, 128), BF16), vmem((group - 1, cv_piece, 128), BF16),
        vmem((row_group, cv_piece, 128), BF16),
        dma((4,)), dma((2, 26)), dma((2, 26)), dma((2, 26)), dma((2, messages)), dma((2, messages)),
    ]
    coarse, fin_up, fin_conv = pl.pallas_call(
        functools.partial(main_kernel, sizes),
        name="halo_compute_reduce",
        out_shape=(
            jax.ShapeDtypeStruct((4, 8, 512), BF16),
            jax.ShapeDtypeStruct((2048, 128), BF16),
            jax.ShapeDtypeStruct((1024, 128), BF16),
        ),
        in_specs=[anywhere] * 4,
        out_specs=(whole, whole, whole),
        scratch_shapes=scratch,
        compiler_params=pltpu.CompilerParams(
            collective_id=0, has_side_effects=True, vmem_limit_bytes=40 * 2**20
        ),
    )(coarse_in, out_grad, up_weight, conv_weight)
    return pl.pallas_call(
        functools.partial(last_kernel, 1.0 / math.sqrt(every_cell)),
        name="scale_outputs",
        out_shape=(
            jax.ShapeDtypeStruct((4, 8, 512), BF16),
            jax.ShapeDtypeStruct((64, C, C), F32),
            jax.ShapeDtypeStruct((27, C, C), F32),
        ),
        in_specs=[whole] * 3,
        out_specs=(whole, whole, whole),
        compiler_params=pltpu.CompilerParams(vmem_limit_bytes=32 * 2**20),
    )(coarse, fin_up, fin_conv)


def solution(mesh):
    sizes = tuple(mesh.shape[a] for a in ("gx", "gy", "gz"))
    in_specs = (P("gx", "gy", "gz"), P("gx", "gy", "gz"), P(), P())
    out_specs = (P("gx", "gy", "gz"), P(), P())
    return jax.shard_map(
        functools.partial(local, sizes), mesh=mesh, in_specs=in_specs, out_specs=out_specs, check_vma=False
    )
```

profile of v0, /device:TPU:1, one launch (start us, length us, event | category | flops | bytes accessed | tf_op | source)
XLA Modules:
  0.0 59.0 jit_solution(612151476579224764)
XLA Ops:
  0.6 0.0 copy-start
  0.6 1.2 %copy-done = bf16[64,64,64]{2,1,0:T(8,128)(2,1)S(1)} copy-done((bf16[64,64,64]{2,1,0:T(8,128)(2,1)S(1)}, bf16[64,64,64]{2,1,0:T(8,128)(2,1)}, u32[]{:S(2)}) %copy-start) | copy-done | bytes 524312
  1.9 0.0 copy-start.1
  1.9 1.0 %copy-done.1 = bf16[27,64,64]{2,1,0:T(8,128)(2,1)S(1)} copy-done((bf16[27,64,64]{2,1,0:T(8,128)(2,1)S(1)}, bf16[27,64,64]{2,1,0:T(8,128)(2,1)}, u32[]{:S(2)}) %copy-start.1) | copy-done | bytes 221208
  2.9 0.0 copy-start.2
  2.9 0.9 %copy-done.2 = bf16[8,16,1024]{2,1,0:T(8,128)(2,1)S(1)} copy-done((bf16[8,16,1024]{2,1,0:T(8,128)(2,1)S(1)}, bf16[8,16,1024]{2,1,0:T(8,128)(2,1)}, u32[]{:S(2)}) %copy-start.2) | copy-done | bytes 262168
  3.8 0.0 copy-start.3
  3.8 0.8 %copy-done.3 = bf16[4,8,512]{2,1,0:T(8,128)(2,1)S(1)} copy-done((bf16[4,8,512]{2,1,0:T(8,128)(2,1)S(1)}, bf16[4,8,512]{2,1,0:T(8,128)(2,1)}, u32[]{:S(2)}) %copy-start.3) | copy-done | bytes 32792
  4.6 52.4 %halo_compute_reduce.1 = (bf16[4,8,512]{2,1,0:T(8,128)(2,1)S(1)}, bf16[2048,128]{1,0:T(8,128)(2,1)S(1)}, bf16[1024,128]{1,0:T(8,128)(2,1)S(1)}) custom-call(bf16[4,8,512]{2,1,0:T(8,128)(2,1)S(1)} %copy-done.3, bf16[8,16,1024]{2,1,0:T(8,128)(2,1)S(1)} %copy-done.2, bf16[64,64,64]{2,1,0:T(8,128)(2,1)S(1)} %copy-done, bf16[27,64,64]{2,1,0:T(8,128)(2,1)S(1)} %copy-done.1), custom_call_target="tpu_custom_call" | custom-call | tf_op jit(solution)/shard_map/halo_compute_reduce/pallas_call | solution.py:452
  57.0 2.0 %scale_outputs.1 = (bf16[4,8,512]{2,1,0:T(8,128)(2,1)}, f32[64,64,64]{2,1,0:T(8,128)}, f32[27,64,64]{2,1,0:T(8,128)}) custom-call(bf16[4,8,512]{2,1,0:T(8,128)(2,1)S(1)} %get-tuple-element.6.coarse, bf16[2048,128]{1,0:T(8,128)(2,1)S(1)} %get-tuple-element.7.fin_up, bf16[1024,128]{1,0:T(8,128)(2,1)S(1)} %get-tuple-element.8.fin_conv), custom_call_target="tpu_custom_call" | custom-call | tf_op jit(solution)/shard_map/scale_outputs/pallas_call | solution.py:467
Async XLA Ops:
  0.6 1.2 %copy-start = (bf16[64,64,64]{2,1,0:T(8,128)(2,1)S(1)}, bf16[64,64,64]{2,1,0:T(8,128)(2,1)}, u32[]{:S(2)}) copy-start(bf16[64,64,64]{2,1,0:T(8,128)(2,1)} %wu_in.1) | copy-start | bytes 1572868
  1.9 1.0 %copy-start.1 = (bf16[27,64,64]{2,1,0:T(8,128)(2,1)S(1)}, bf16[27,64,64]{2,1,0:T(8,128)(2,1)}, u32[]{:S(2)}) copy-start(bf16[27,64,64]{2,1,0:T(8,128)(2,1)} %wc_in.1) | copy-start | bytes 663556
  2.9 0.9 %copy-start.2 = (bf16[8,16,1024]{2,1,0:T(8,128)(2,1)S(1)}, bf16[8,16,1024]{2,1,0:T(8,128)(2,1)}, u32[]{:S(2)}) copy-start(bf16[8,16,1024]{2,1,0:T(8,128)(2,1)} %g_in.1) | copy-start | bytes 786436
  3.8 0.8 %copy-start.3 = (bf16[4,8,512]{2,1,0:T(8,128)(2,1)S(1)}, bf16[4,8,512]{2,1,0:T(8,128)(2,1)}, u32[]{:S(2)}) copy-start(bf16[4,8,512]{2,1,0:T(8,128)(2,1)} %u_in.1) | copy-start | bytes 98308
where the time goes:
time: 59.3 us; the launch traced here: 59 us
  Pallas kernels  54.4 us (92%)
  local copies, waits for them, and re-layouts  3.94 us (7%)
  between operations  0.65 us (1%)
    pallas_call x1, Pallas kernels, local(): pl.pallas_call(functools.partial(main_kernel, sizes), name='halo_compute_...  52.4 us
    unnamed x8, local copies, waits for them, and re-layouts  3.94 us
    pallas_call x1, Pallas kernels, local(): pl.pallas_call(functools.partial(last_kernel, 1.0 / math.sqrt(every_cell)...  1.98 us

commit v1 on v0

v1 whole, which is shorter than its diff:
```python
import functools
import itertools
import math

import jax
import jax.numpy as jnp
from jax import lax
from jax.experimental import pallas as pl
from jax.experimental.pallas import tpu as pltpu
from jax.sharding import PartitionSpec as P

MESH = pl.DeviceIdType.MESH
F32 = jnp.float32
BF16 = jnp.bfloat16
C = 64
gelu_coef = 0.7978845608
gelu_cube = 0.044715
taps_by_parity = (((0, 3), (1, 1)), ((1, 2), (2, 0)))
NEIGHBOURS = sorted((o for o in itertools.product((-1, 0, 1), repeat=3) if any(o)), key=lambda o: -sum(map(abs, o)) - 9 * abs(o[0]))
G_PLANES = [0, 3, 4, 5, 6, 7, 8, 9, 12, 15]
U_PLANES = [1, 2, 10, 11, 13, 14]


def nt(left, right):
    return lax.dot_general(left, right, (((1,), (1,)), ((), ())), preferred_element_type=F32)


def nn(left, right):
    return jnp.dot(left, right, preferred_element_type=F32)


class Place:
    def __init__(self, sizes):
        self.sizes = sizes
        self.gx, self.gy, self.gz = (lax.axis_index(a) for a in ("gx", "gy", "gz"))
        self.nz, self.nx, self.ny = sizes[0] // 2, sizes[1], sizes[2]
        self.low = sizes[2] // 2
        self.z, self.x = self.gx // 2, self.gy
        self.y = self.gx % 2 * self.low + self.gz // 2
        self.core = self.gz % 2
        self.index = self.z * self.nx + self.x
        self.group = self.nz * self.nx
        self.row_group = 2 * self.low

    def neighbour(self, o):
        me = (self.gx, self.gy, self.gz)
        return tuple(lax.rem(m + d + n, n) for m, d, n in zip(me, o, self.sizes))

    def sibling(self):
        return (self.gx, self.gy, self.gz + 1 - 2 * self.core)

    def in_group(self, dz, dx):
        z, x = lax.rem(self.z + dz, self.nz), lax.rem(self.x + dx, self.nx)
        return (z * 2 + self.gx % 2, x, self.gz), z * self.nx + x

    def in_row(self, dy):
        y = lax.rem(self.y + dy, self.row_group)
        return (self.z * 2 + y // self.low, self.x, y % self.low * 2 + self.core)

    def group_steps(self):
        far = lambda o: -min(o[0], self.nz - o[0]) - min(o[1], self.nx - o[1])
        return sorted((o for o in itertools.product(range(self.nz), range(self.nx)) if any(o)), key=far)


def remote(src, dst, send, recv, device):
    return pltpu.make_async_remote_copy(
        src_ref=src, dst_ref=dst, send_sem=send, recv_sem=recv, device_id=device, device_id_type=MESH
    )


def halo(place, xt, edge, faces, extra, ys, yt, ct, ctr, send, recv):
    copies = {}
    planes, lanes = xt.shape[0], xt.shape[2] - 256
    inner = planes - 2 * edge
    for i, (ox, oy, oz) in enumerate(NEIGHBOURS):
        device = place.neighbour((ox, oy, oz))
        zs, zd = {
            0: (pl.ds(0, lanes), pl.ds(128, lanes)),
            1: (pl.ds(lanes - 128, 128), pl.ds(0, 128)),
            -1: (pl.ds(0, 128), pl.ds(lanes + 128, 128)),
        }[oz]
        side, end = (1 - oy) // 2, (1 - ox) // 2
        if oy == 0:
            zs = pl.ds(zs.start + 128, zs.size)
            if ox == 0:
                xs, xd = pl.ds(edge, inner), pl.ds(edge, inner)
            elif oz == 0:
                xs, xd = faces[end]
            else:
                xs, xd = (
                    (pl.ds(inner, edge), pl.ds(0, edge)),
                    (pl.ds(edge, edge), pl.ds(planes - edge, edge)),
                )[end]
            src, dst = xt.at[xs, :, zs], xt.at[xd, :, zd]
        elif ox == 0:
            src, dst = ys.at[side, :, zs], yt.at[side, :, zd]
        else:
            src, dst = ct.at[end, side], ctr.at[end, side, 1 - oz]
        copies[ox, oy, oz] = remote(src, dst, send.at[i], recv.at[i], device)
        if extra is not None and ox != 0 and (oy, oz) == (0, 0):
            source, target = extra
            copies[ox, None, None] = remote(
                source.at[end], target.at[end], send.at[26 + end], recv.at[26 + end], device
            )
    for copy in copies.values():
        copy.start()
    return copies


class AllReduce:
    def __init__(self, place, total, fin, r1, s, r2, r3, sems):
        self.place, self.total, self.fin = place, total, fin
        self.r1, self.s, self.r2, self.r3, self.sems = r1, s, r2, r3, sems
        self.half = total.shape[0] // 2
        self.piece = self.half // place.group
        self.used = 0
        self.flight, self.sent = [], []

    def send(self, src, dst, device):
        i = self.used
        self.used += 1
        copy = remote(src, dst, self.sems.at[0, i], self.sems.at[1, i], device)
        copy.start()
        self.flight.append(copy)

    def arrive(self):
        for copy in self.flight:
            copy.wait_recv()
        self.sent += self.flight
        self.flight = []

    def finish(self):
        self.arrive()
        self.store.wait()
        for copy in self.sent:
            copy.wait_send()

    def mine(self, index, size):
        return pl.ds(pl.multiple_of(index * size, size), size)

    def pair(self):
        p = self.place
        self.send(self.total.at[self.mine(1 - p.core, self.half)], self.r1, p.sibling())

    def scatter(self):
        p = self.place
        self.arrive()
        self.s[...] = (self.total[self.mine(p.core, self.half), :] + self.r1[...]).astype(BF16)
        for k, o in enumerate(p.group_steps()):
            device, index = p.in_group(*o)
            self.send(self.s.at[self.mine(index, self.piece)], self.r2.at[k], device)

    def exchange(self):
        p = self.place
        self.arrive()
        total = self.s[self.mine(p.index, self.piece), :].astype(F32)
        for k in range(p.group - 1):
            total = total + self.r2[k].astype(F32)
        self.r3[p.y] = total.astype(BF16)
        for dy in range(1, p.row_group):
            self.send(self.r3.at[p.y], self.r3.at[p.y], p.in_row(dy))

    def spot(self):
        p = self.place
        return pl.ds(pl.multiple_of(p.core * self.half + p.index * self.piece, self.piece), self.piece)

    def gather(self):
        p = self.place
        self.arrive()
        total = self.r3[0].astype(F32)
        for k in range(1, p.row_group):
            total = total + self.r3[k].astype(F32)
        self.fin[self.spot(), :] = total.astype(BF16)
        for o in p.group_steps():
            device, _ = p.in_group(*o)
            self.send(self.fin.at[self.spot()], self.fin.at[self.spot()], device)

    def share(self, out, sem):
        p = self.place
        self.arrive()
        spot = self.mine(p.core, self.half)
        self.send(self.fin.at[spot], out.at[spot], p.sibling())
        self.store = pltpu.make_async_copy(self.fin.at[spot], out.at[spot], sem)
        self.store.start()


def main_kernel(
    sizes, u_in, g_in, wu_in, wc_in,
    coarse_out, out_up, out_conv,
    ub, wu, wc, ue, ue1, uc, uce, xt, ysf, ys, yt, ct, ctr, ctf, yf, yr, ge, ga, gb,
    wp, cw, w3, uw, uwt, pre, slope, ht, gp,
    pxt, pys, pyt, pct, pctr, pyf, pyr, pe, co, gc,
    a_up, a_conv, fin_up, fin_conv, up_r1, up_s, up_r2, up_r3, cv_r1, cv_s, cv_r2, cv_r3,
    local_sems, g_sems, p_sems, up_sems, cv_sems,
):
    place = Place(sizes)
    barrier = pltpu.get_barrier_semaphore()
    partners = [place.neighbour(o) for o in NEIGHBOURS]
    partners += [place.in_group(*o)[0] for o in place.group_steps()]
    partners += [place.in_row(dy) for dy in range(1, place.row_group)]
    partners += [place.sibling()]
    for device in partners:
        pl.semaphore_signal(barrier, inc=1, device_id=device, device_id_type=MESH)
    loads = [
        pltpu.make_async_copy(u_in, ub, local_sems.at[0]),
        pltpu.make_async_copy(g_in.at[pl.ds(0, 7)], xt.at[pl.ds(3, 7), :, pl.ds(128, 1024)], local_sems.at[1]),
        pltpu.make_async_copy(wu_in, wu, local_sems.at[2]),
        pltpu.make_async_copy(wc_in, wc, local_sems.at[3]),
        pltpu.make_async_copy(g_in.at[7], xt.at[12, :, pl.ds(128, 1024)], local_sems.at[4]),
    ]
    for load in loads:
        load.start()

    zero_rows = jnp.zeros((4, 1024), F32)
    for side in range(2):
        ysf[side, 12:16, :] = zero_rows
    loads[0].wait()
    for x in range(4):
        rows = ub[x].astype(F32)
        ue[1 + x, 8:16, 128:640] = rows
        plane = U_PLANES[1 + x]
        for z, lane in ((0, 128), (384, 1024)):
            both = jnp.concatenate([rows[:, z : z + 128], rows[:, z : z + 128]], axis=0)
            xt[plane, :, lane : lane + 128] = both.astype(BF16)
        if x in (0, 3):
            uc[(3 - x) // 3] = jnp.concatenate([rows[:, 0:256], rows[:, 256:512]], axis=0).astype(BF16)
        for side, row in ((0, 7), (1, 0)):
            ysf[side, 8 + x : 9 + x, 0:256] = rows[row : row + 1, 0:256]
            ysf[side, 8 + x : 9 + x, 256:768] = jnp.zeros((1, 512), F32)
            ysf[side, 8 + x : 9 + x, 768:1024] = rows[row : row + 1, 256:512]
    loads[1].wait()
    loads[4].wait()
    for x in range(8):
        block = xt[G_PLANES[1 + x], :, 128:1152].astype(F32)
        ysf[0, x : x + 1, :] = block[15:16]
        ysf[1, x : x + 1, :] = block[0:1]
    for side in range(2):
        ys[side] = ysf[side].astype(BF16)
        for end, x, xc in ((0, 7, 3), (1, 0, 0)):
            ctf[end, side, 0, 8:16, :] = jnp.zeros((8, 128), F32)
            for j in range(8):
                ctf[end, side, 0, j : j + 1, :] = ysf[side, x : x + 1, 128 * j : 128 * j + 128]
            for j, lane in enumerate((0, 128, 768, 896)):
                ctf[end, side, 0, 8 + j : 9 + j, :] = ysf[side, 8 + xc : 9 + xc, lane : lane + 128]
            ct[end, side] = ctf[end, side, 0].astype(BF16)
    pl.semaphore_wait(barrier, len(partners))
    copies = halo(
        place, xt, 2, ((12, 0), (3, 15)), (uc, uce), ys, yt, ct, ctr, g_sems.at[0], g_sems.at[1]
    )

    loads[2].wait()
    loads[3].wait()
    blank = jnp.zeros((C, C), BF16)
    for q in range(16):
        k0, k1, k2, k3 = (wu[4 * q + k] for k in range(4))
        wp[q, 0:64, :] = jnp.concatenate([k3, blank], axis=1)
        wp[q, 64:128, :] = jnp.concatenate([k1, k2], axis=1)
        wp[q, 128:192, :] = jnp.concatenate([blank, k0], axis=1)
        wp[q, 192:256, :] = jnp.zeros((C, 2 * C), BF16)
        w3[q, :, 0:128] = jnp.concatenate([k0, k1], axis=1)
        w3[q, :, 128:256] = jnp.concatenate([k2, k3], axis=1)
    for dx in range(3):
        for dy in range(3):
            d0, d1, d2 = (wc[9 * dx + 3 * dy + d] for d in range(3))
            tap = jnp.concatenate(
                [
                    jnp.concatenate([d2, d1, d0, blank], axis=1),
                    jnp.concatenate([blank, d2, d1, d0], axis=1),
                ],
                axis=0,
            )
            for py in range(2):
                lane = 256 * (4 * dx + py - dy + 2)
                cw[128 * py : 128 * py + 128, lane : lane + 256] = tap
        cw[128:256, 1024 * dx : 1024 * dx + 256] = jnp.zeros((128, 256), BF16)
        cw[0:128, 1024 * dx + 768 : 1024 * dx + 1024] = jnp.zeros((128, 256), BF16)

    for copy in copies.values():
        copy.wait_recv()
    ctf[...] = ctr[...].astype(F32)
    for side in range(2):
        yf[side, 0:16, :] = yt[side].astype(F32)
        for end in range(2):
            for j in range(10):
                tile, row = (0, 7) if j == 0 else (2, 0) if j == 9 else (1, j - 1)
                yf[side, 16 + end : 17 + end, 128 * j : 128 * j + 128] = ctf[end, side, tile, row : row + 1, :]
            for j in range(6):
                tile, row = (0, 11) if j == 0 else (2, 8) if j == 5 else (1, 7 + j)
                ue[5 * end, 7 + 9 * side : 8 + 9 * side, 128 * j : 128 * j + 128] = ctf[
                    end, side, tile, row : row + 1, :
                ]
        for x in range(1, 5):
            row = slice(7 + x, 8 + x)
            ue[x, 7 + 9 * side : 8 + 9 * side, 0:384] = yf[side, row, 0:384]
            ue[x, 7 + 9 * side : 8 + 9 * side, 384:768] = yf[side, row, 896:1280]
    for end in range(2):
        face = uce[end].astype(F32)
        ue[5 * end, 8:16, 128:384] = face[0:8]
        ue[5 * end, 8:16, 384:640] = face[8:16]
    for x in range(6):
        ue[x, 8:16, 0:128] = xt[U_PLANES[x], :, 0:128].astype(F32)[0:8]
        ue[x, 8:16, 640:768] = xt[U_PLANES[x], :, 1152:1280].astype(F32)[0:8]
    for x in range(6):
        ue1[x] = pltpu.roll(ue[x], 768 - 64, 1)[:, :640]
    for sx in range(3):
        for sy in range(3):
            rows = []
            for zc in range(8):
                if zc % 2:
                    part = ue[sx : sx + 4, 7 + sy : 15 + sy, 64 * (zc + 1) : 64 * (zc + 1) + 256]
                else:
                    part = ue1[sx : sx + 4, 7 + sy : 15 + sy, 64 * zc : 64 * zc + 256]
                rows.append(part.reshape(32, 256))
            window = jnp.concatenate(rows, axis=0)
            uw[3 * sx + sy] = window.astype(BF16)
            uwt[3 * sx + sy] = window.T.astype(BF16)[:192]

    for px in range(2):
        for py in range(2):
            total = None
            for sx, kx in taps_by_parity[px]:
                for sy, ky in taps_by_parity[py]:
                    part = nn(uw[3 * sx + sy], wp[4 * kx + ky])
                    total = part if total is None else total + part
            total = total.reshape(8, 4, 8, 128)
            for xc in range(4):
                pre[:, 2 * xc + px, :, 128 * py : 128 * py + 128] = total[:, xc]
    for zc in range(0, 8, 2):
        v = pre[zc : zc + 2].reshape(128, 256)
        square = v * v
        tangent = jnp.tanh(gelu_coef * (v + gelu_cube * (square * v)))
        hidden = 0.5 * v * (1.0 + tangent)
        ht[:, 64 * zc : 64 * zc + 128] = hidden.T.astype(BF16)
        slope[64 * zc : 64 * zc + 128, :] = 0.5 * (1.0 + tangent) + 0.5 * v * (
            1.0 - tangent * tangent
        ) * gelu_coef * (1.0 + 3.0 * gelu_cube * square)

    turn = xt.shape[2] - 64
    for side in range(2):
        yr[side] = pltpu.roll(yf[side], turn, 1)[:, :1152]
    for x in range(10):
        turned = pltpu.roll(xt[G_PLANES[x]].astype(F32), turn, 1)
        row = 16 if x == 0 else 17 if x == 9 else x - 1
        for pair in range(9):
            lanes = slice(128 * pair, 128 * pair + 128)
            ge[pair, x, 8:24, :] = turned[:, lanes]
            ge[pair, x, 7:8, :] = yr[0, row : row + 1, lanes]
            ge[pair, x, 24:25, :] = yr[1, row : row + 1, lanes]
    for pair in range(9):
        for ky in range(4):
            rows = [ge[pair, x, pl.ds(7 + ky, 8, stride=2), :] for x in range(10)]
            ga[ky, pair] = jnp.concatenate(rows, axis=0).astype(BF16)
            gb[ky, pair] = jnp.concatenate(rows[1:9], axis=0).astype(BF16)

    def window(dx, ky):
        parts = []
        for zc in range(8):
            if dx == 1:
                pairs = [gb[ky, zc + s] for s in range(2)]
            else:
                first = 16 - 8 * dx
                pairs = [ga[ky, zc + s, first : first + 64] for s in range(2)]
            parts.append(jnp.concatenate(pairs, axis=1))
        return jnp.concatenate(parts, axis=0)

    total = None
    for dx in range(3):
        for ky in range(4):
            lane = 256 * (4 * dx + ky)
            part = nt(window(dx, ky), cw[:, lane : lane + 256])
            total = part if total is None else total + part
    gp[...] = (total * slope[...]).astype(BF16).astype(F32).reshape(8, 8, 8, 256)

    low = lax.broadcasted_iota(jnp.int32, (C, 2 * C), 1) < C
    for px in range(2):
        for py in range(2):
            rows = [gp[:, 2 * xc + px, :, 128 * py : 128 * py + 128] for xc in range(4)]
            grad = jnp.stack(rows, axis=1).reshape(256, 128).astype(BF16)
            for sx, kx in taps_by_parity[px]:
                for sy, ky in taps_by_parity[py]:
                    q = 4 * kx + ky
                    part = nn(uwt[3 * sx + sy], grad)
                    a_up[128 * q : 128 * q + 64, :] = part[64:128]
                    a_up[128 * q + 64 : 128 * q + 128, :] = jnp.where(low, part[0:64], part[128:192])
    up = AllReduce(place, a_up, fin_up, up_r1, up_s, up_r2, up_r3, up_sems)
    up.pair()

    for dx in range(3):
        products = [
            nn(ht[0:128, :], window(dx, 0)),
            nn(ht[...], window(dx, 1)),
            nn(ht[...], window(dx, 2)),
            nn(ht[128:256, :], window(dx, 3)),
        ]
        for dy in range(3):
            part = products[2 - dy][:128] + products[3 - dy][-128:]
            gc[3 * dx + dy] = part[:64] + pltpu.roll(part[64:], 256 - 64, 1)
    for t in range(9):
        a_conv[64 * t : 64 * t + 64, :] = gc[t, :, 0:128]
    for m in range(5):
        if m < 4:
            other = pltpu.roll(gc[2 * m + 1, :, 128:256], 64, 1)
            joined = jnp.where(low, gc[2 * m, :, 128:256], other)
        else:
            joined = gc[8, :, 128:256]
        a_conv[64 * (9 + m) : 64 * (10 + m), :] = joined
    a_conv[896:1024, :] = jnp.zeros((128, 128), F32)
    conv = AllReduce(place, a_conv, fin_conv, cv_r1, cv_s, cv_r2, cv_r3, cv_sems)
    conv.pair()
    up.scatter()
    conv.scatter()

    for x in range(8):
        for zc in range(8):
            block = gp[zc, x]
            rows = jnp.concatenate([block[:, 0:128], block[:, 128:256]], axis=0)
            pxt[1 + x, :, 128 * zc + 128 : 128 * zc + 256] = rows.astype(BF16)
            pys[0, x : x + 1, 128 * zc : 128 * zc + 128] = gp[zc, x, 7:8, 128:256]
            pys[1, x : x + 1, 128 * zc : 128 * zc + 128] = gp[zc, x, 0:1, 0:128]
            if x in (0, 7):
                pct[(7 - x) // 7, 0, zc : zc + 1, :] = gp[zc, x, 7:8, 128:256]
                pct[(7 - x) // 7, 1, zc : zc + 1, :] = gp[zc, x, 0:1, 0:128]
    p_copies = halo(
        place, pxt, 1, ((8, 0), (1, 9)), None, pys, pyt, pct, pctr, p_sems.at[0], p_sems.at[1]
    )
    up.exchange()
    conv.exchange()

    for copy in p_copies.values():
        copy.wait_recv()
    for side in range(2):
        pyf[side, 0:8, :] = pyt[side]
        for end in range(2):
            for j in range(10):
                tile, row = (0, 7) if j == 0 else (2, 0) if j == 9 else (1, j - 1)
                pyf[side, 8 + end : 9 + end, 128 * j : 128 * j + 128] = pctr[end, side, tile, row : row + 1, :]
        pyr[side] = pltpu.roll(pyf[side], turn, 1)[:, :1152]
    for x in range(10):
        turned = pltpu.roll(pxt[x].astype(F32), turn, 1)
        row = 8 if x == 0 else 9 if x == 9 else x - 1
        for pair in range(9):
            lanes = slice(128 * pair, 128 * pair + 128)
            pe[pair, x, 0, 8:16, :] = turned[0:8, lanes]
            pe[pair, x, 1, 8:16, :] = turned[8:16, lanes]
            pe[pair, x, 0, 16:17, :] = pyr[1, row : row + 1, lanes]
            pe[pair, x, 1, 7:8, :] = pyr[0, row : row + 1, lanes]
    total = None
    for kx in range(4):
        for ky in range(4):
            parity, first = ((1, 7), (0, 8), (1, 8), (0, 9))[ky]
            pairs = [
                jnp.concatenate([pe[pair, 2 * xc + kx, parity, first : first + 8, :] for xc in range(4)], axis=0)
                for pair in range(9)
            ]
            rows = [jnp.concatenate([pairs[zc], pairs[zc + 1]], axis=1) for zc in range(8)]
            part = nt(jnp.concatenate(rows, axis=0).astype(BF16), w3[4 * kx + ky])
            total = part if total is None else total + part
        if kx == 1:
            up.gather()
    conv.gather()
    total = total.reshape(8, 4, 8, C)
    for zc in range(0, 8, 2):
        co[:, :, 64 * zc : 64 * zc + 128] = jnp.concatenate([total[zc], total[zc + 1]], axis=2).astype(BF16)
    store = pltpu.make_async_copy(co, coarse_out, local_sems.at[5])
    store.start()
    up.share(out_up, local_sems.at[6])
    conv.share(out_conv, local_sems.at[7])
    up.finish()
    conv.finish()
    store.wait()
    for copy in [*copies.values(), *p_copies.values()]:
        copy.wait_send()


def last_kernel(
    factor, coarse, in_up, in_conv, coarse_out, up_out, conv_out, fin_up, fin_conv, up, conv, in_sems, out_sems
):
    through = pltpu.make_async_copy(coarse, coarse_out, out_sems.at[5])
    through.start()
    parts = [pl.ds(512 * i, 512) for i in range(4)]
    loads = [pltpu.make_async_copy(in_up.at[p], fin_up.at[p], in_sems.at[i]) for i, p in enumerate(parts)]
    loads.append(pltpu.make_async_copy(in_conv, fin_conv, in_sems.at[4]))
    for load in loads:
        load.start()
    stores = []
    for i in range(4):
        loads[i].wait()
        for q in range(4 * i, 4 * i + 4):
            first = fin_up[128 * q : 128 * q + 64, :].astype(F32) * factor
            second = fin_up[128 * q + 64 : 128 * q + 128, :].astype(F32) * factor
            up[4 * q + 1] = first[:, :C]
            up[4 * q + 2] = first[:, C:]
            up[4 * q + 3] = second[:, :C]
            up[4 * q] = second[:, C:]
        part = pl.ds(16 * i, 16)
        stores.append(pltpu.make_async_copy(up.at[part], up_out.at[part], out_sems.at[i]))
        stores[-1].start()
    loads[4].wait()
    for t in range(9):
        both = fin_conv[64 * t : 64 * t + 64, :].astype(F32) * factor
        conv[3 * t + 2] = both[:, :C]
        conv[3 * t + 1] = both[:, C:]
        m = t // 2
        rest = fin_conv[64 * (9 + m) : 64 * (10 + m), :].astype(F32) * factor
        conv[3 * t] = rest[:, C:] if t % 2 else rest[:, :C]
    stores.append(pltpu.make_async_copy(conv, conv_out, out_sems.at[4]))
    stores[-1].start()
    for store in stores:
        store.wait()
    through.wait()


def local(sizes, coarse_in, out_grad, up_weight, conv_weight):
    every_cell = 2048 * sizes[0] * sizes[1] * sizes[2]
    group = sizes[0] // 2 * sizes[1]
    row_group = sizes[2] // 2 * 2
    up_piece, cv_piece = 1024 // group, 512 // group
    messages = 2 + 2 * (group - 1) + row_group - 1
    vmem = pltpu.VMEM
    dma = pltpu.SemaphoreType.DMA
    anywhere = pl.BlockSpec(memory_space=pl.ANY)
    scratch = [
        vmem((4, 8, 512), BF16), vmem((64, C, C), BF16), vmem((27, C, C), BF16),
        vmem((6, 24, 768), F32), vmem((6, 24, 640), F32), vmem((2, 16, 256), BF16), vmem((2, 16, 256), BF16),
        vmem((16, 16, 1280), BF16), vmem((2, 16, 1024), F32), vmem((2, 16, 1024), BF16),
        vmem((2, 16, 1280), BF16), vmem((2, 2, 16, 128), BF16), vmem((2, 2, 3, 16, 128), BF16),
        vmem((2, 2, 3, 16, 128), F32), vmem((2, 24, 1280), F32), vmem((2, 24, 1152), F32),
        vmem((9, 10, 32, 128), F32), vmem((4, 9, 80, 128), BF16), vmem((4, 9, 64, 128), BF16),
        vmem((16, 256, 128), BF16), vmem((256, 3072), BF16), vmem((16, 64, 256), BF16),
        vmem((9, 256, 256), BF16), vmem((9, 192, 256), BF16),
        vmem((8, 8, 8, 256), F32), vmem((512, 256), F32), vmem((256, 512), BF16), vmem((8, 8, 8, 256), F32),
        vmem((10, 16, 1280), BF16), vmem((2, 8, 1024), F32), vmem((2, 8, 1280), F32),
        vmem((2, 2, 8, 128), F32), vmem((2, 2, 3, 8, 128), F32), vmem((2, 16, 1280), F32),
        vmem((2, 16, 1152), F32), vmem((9, 10, 2, 24, 128), F32), vmem((4, 8, 512), BF16),
        vmem((9, 64, 256), F32),
        vmem((2048, 128), F32), vmem((1024, 128), F32), vmem((2048, 128), BF16), vmem((1024, 128), BF16),
        vmem((1024, 128), F32), vmem((1024, 128), BF16), vmem((group - 1, up_piece, 128), BF16),
        vmem((row_group, up_piece, 128), BF16),
        vmem((512, 128), F32), vmem((512, 128), BF16), vmem((group - 1, cv_piece, 128), BF16),
        vmem((row_group, cv_piece, 128), BF16),
        dma((8,)), dma((2, 28)), dma((2, 26)), dma((2, messages)), dma((2, messages)),
    ]
    coarse, fin_up, fin_conv = pl.pallas_call(
        functools.partial(main_kernel, sizes),
        name="halo_compute_reduce",
        out_shape=(
            jax.ShapeDtypeStruct((4, 8, 512), BF16),
            jax.ShapeDtypeStruct((2048, 128), BF16),
            jax.ShapeDtypeStruct((1024, 128), BF16),
        ),
        in_specs=[anywhere] * 4,
        out_specs=(anywhere,) * 3,
        scratch_shapes=scratch,
        compiler_params=pltpu.CompilerParams(
            collective_id=0, has_side_effects=True, vmem_limit_bytes=60 * 2**20
        ),
    )(coarse_in, out_grad, up_weight, conv_weight)
    return pl.pallas_call(
        functools.partial(last_kernel, 1.0 / math.sqrt(every_cell)),
        name="scale_outputs",
        out_shape=(
            jax.ShapeDtypeStruct((4, 8, 512), BF16),
            jax.ShapeDtypeStruct((64, C, C), F32),
            jax.ShapeDtypeStruct((27, C, C), F32),
        ),
        in_specs=[anywhere] * 3,
        out_specs=(anywhere,) * 3,
        scratch_shapes=[
            vmem((2048, 128), BF16), vmem((1024, 128), BF16), vmem((64, C, C), F32), vmem((27, C, C), F32),
            dma((5,)), dma((6,)),
        ],
        compiler_params=pltpu.CompilerParams(vmem_limit_bytes=60 * 2**20),
    )(coarse, fin_up, fin_conv)


def solution(mesh):
    sizes = tuple(mesh.shape[a] for a in ("gx", "gy", "gz"))
    in_specs = (P("gx", "gy", "gz"), P("gx", "gy", "gz"), P(), P())
    out_specs = (P("gx", "gy", "gz"), P(), P())
    return jax.shard_map(
        functools.partial(local, sizes), mesh=mesh, in_specs=in_specs, out_specs=out_specs, check_vma=False
    )
```

time: 59.3 us -> 47.2 us (0.80)
  Pallas kernels: 54.4 us -> 46.4 us
  local copies, waits for them, and re-layouts: 3.94 us -> 0 us
    pallas_call x1, Pallas kernels: 52.4 us -> 43.7 us  [local(): pl.pallas_call(functools.partial(main_kernel, sizes), name='halo_compute_...]
    unnamed x8 -> x0, local copies, waits for them, and re-layouts: 3.94 us -> none
    pallas_call x1, Pallas kernels: 1.98 us -> 2.74 us  [local(): pl.pallas_call(functools.partial(last_kernel, 1.0 / math.sqrt(every_cell)...]
where the time goes in v1:
time: 47.2 us; the launch traced here: 47 us
  Pallas kernels  46.4 us (98%)
  between operations  0.64 us (1%)
    pallas_call x1, Pallas kernels, local(): pl.pallas_call(functools.partial(main_kernel, sizes), name='halo_compute_...  43.7 us
    pallas_call x1, Pallas kernels, local(): pl.pallas_call(functools.partial(last_kernel, 1.0 / math.sqrt(every_cell)...  2.74 us

profile of v1, /device:TPU:1, one launch (start us, length us, event | category | flops | bytes accessed | tf_op | source)
XLA Modules:
  0.0 47.0 jit_solution(11494901239787908387)
XLA Ops:
  0.6 43.7 %halo_compute_reduce.1 = (bf16[4,8,512]{2,1,0:T(8,128)(2,1)}, bf16[2048,128]{1,0:T(8,128)(2,1)}, bf16[1024,128]{1,0:T(8,128)(2,1)}) custom-call(bf16[4,8,512]{2,1,0:T(8,128)(2,1)} %u_in.1, bf16[8,16,1024]{2,1,0:T(8,128)(2,1)} %g_in.1, bf16[64,64,64]{2,1,0:T(8,128)(2,1)} %wu_in.1, bf16[27,64,64]{2,1,0:T(8,128)(2,1)} %wc_in.1), custom_call_target="tpu_custom_call" | custom-call | tf_op jit(solution)/shard_map/halo_compute_reduce/pallas_call | solution.py:543
  44.3 2.7 %scale_outputs.1 = (bf16[4,8,512]{2,1,0:T(8,128)(2,1)}, f32[64,64,64]{2,1,0:T(8,128)}, f32[27,64,64]{2,1,0:T(8,128)}) custom-call(bf16[4,8,512]{2,1,0:T(8,128)(2,1)} %get-tuple-element.6.coarse, bf16[2048,128]{1,0:T(8,128)(2,1)} %get-tuple-element.7.in_up, bf16[1024,128]{1,0:T(8,128)(2,1)} %get-tuple-element.8.in_conv), custom_call_target="tpu_custom_call" | custom-call | tf_op jit(solution)/shard_map/scale_outputs/pallas_call | solution.py:558

commit v2 on v1

--- a/solution.py
+++ b/solution.py
@@ -16,7 +16,7 @@
 gelu_coef = 0.7978845608
 gelu_cube = 0.044715
 taps_by_parity = (((0, 3), (1, 1)), ((1, 2), (2, 0)))
-NEIGHBOURS = sorted((o for o in itertools.product((-1, 0, 1), repeat=3) if any(o)), key=lambda o: -sum(map(abs, o)) - 9 * abs(o[0]))
+NEIGHBOURS = sorted((o for o in itertools.product((-1, 0, 1), repeat=3) if any(o)), key=lambda o: (-abs(o[0]), sum(map(abs, o))))
 G_PLANES = [0, 3, 4, 5, 6, 7, 8, 9, 12, 15]
 U_PLANES = [1, 2, 10, 11, 13, 14]
 
@@ -138,9 +138,11 @@
     def mine(self, index, size):
         return pl.ds(pl.multiple_of(index * size, size), size)
 
-    def pair(self):
+    def pair(self, part=0, parts=1):
         p = self.place
-        self.send(self.total.at[self.mine(1 - p.core, self.half)], self.r1, p.sibling())
+        size = self.half // parts
+        rows = pl.ds(pl.multiple_of((1 - p.core) * self.half + part * size, size), size)
+        self.send(self.total.at[rows], self.r1.at[pl.ds(part * size, size)], p.sibling())
 
     def scatter(self):
         p = self.place
@@ -204,9 +206,9 @@
     loads = [
         pltpu.make_async_copy(u_in, ub, local_sems.at[0]),
         pltpu.make_async_copy(g_in.at[pl.ds(0, 7)], xt.at[pl.ds(3, 7), :, pl.ds(128, 1024)], local_sems.at[1]),
-        pltpu.make_async_copy(wu_in, wu, local_sems.at[2]),
-        pltpu.make_async_copy(wc_in, wc, local_sems.at[3]),
-        pltpu.make_async_copy(g_in.at[7], xt.at[12, :, pl.ds(128, 1024)], local_sems.at[4]),
+        pltpu.make_async_copy(g_in.at[7], xt.at[12, :, pl.ds(128, 1024)], local_sems.at[2]),
+        pltpu.make_async_copy(wu_in, wu, local_sems.at[3]),
+        pltpu.make_async_copy(wc_in, wc, local_sems.at[4]),
     ]
     for load in loads:
         load.start()
@@ -229,7 +231,7 @@
             ysf[side, 8 + x : 9 + x, 256:768] = jnp.zeros((1, 512), F32)
             ysf[side, 8 + x : 9 + x, 768:1024] = rows[row : row + 1, 256:512]
     loads[1].wait()
-    loads[4].wait()
+    loads[2].wait()
     for x in range(8):
         block = xt[G_PLANES[1 + x], :, 128:1152].astype(F32)
         ysf[0, x : x + 1, :] = block[15:16]
@@ -248,8 +250,8 @@
         place, xt, 2, ((12, 0), (3, 15)), (uc, uce), ys, yt, ct, ctr, g_sems.at[0], g_sems.at[1]
     )
 
-    loads[2].wait()
     loads[3].wait()
+    loads[4].wait()
     blank = jnp.zeros((C, C), BF16)
     for q in range(16):
         k0, k1, k2, k3 = (wu[4 * q + k] for k in range(4))
@@ -363,28 +365,7 @@
             parts.append(jnp.concatenate(pairs, axis=1))
         return jnp.concatenate(parts, axis=0)
 
-    total = None
-    for dx in range(3):
-        for ky in range(4):
-            lane = 256 * (4 * dx + ky)
-            part = nt(window(dx, ky), cw[:, lane : lane + 256])
-            total = part if total is None else total + part
-    gp[...] = (total * slope[...]).astype(BF16).astype(F32).reshape(8, 8, 8, 256)
-
     low = lax.broadcasted_iota(jnp.int32, (C, 2 * C), 1) < C
-    for px in range(2):
-        for py in range(2):
-            rows = [gp[:, 2 * xc + px, :, 128 * py : 128 * py + 128] for xc in range(4)]
-            grad = jnp.stack(rows, axis=1).reshape(256, 128).astype(BF16)
-            for sx, kx in taps_by_parity[px]:
-                for sy, ky in taps_by_parity[py]:
-                    q = 4 * kx + ky
-                    part = nn(uwt[3 * sx + sy], grad)
-                    a_up[128 * q : 128 * q + 64, :] = part[64:128]
-                    a_up[128 * q + 64 : 128 * q + 128, :] = jnp.where(low, part[0:64], part[128:192])
-    up = AllReduce(place, a_up, fin_up, up_r1, up_s, up_r2, up_r3, up_sems)
-    up.pair()
-
     for dx in range(3):
         products = [
             nn(ht[0:128, :], window(dx, 0)),
@@ -407,8 +388,28 @@
     a_conv[896:1024, :] = jnp.zeros((128, 128), F32)
     conv = AllReduce(place, a_conv, fin_conv, cv_r1, cv_s, cv_r2, cv_r3, cv_sems)
     conv.pair()
-    up.scatter()
+
+    total = None
+    for dx in range(3):
+        for ky in range(4):
+            lane = 256 * (4 * dx + ky)
+            part = nt(window(dx, ky), cw[:, lane : lane + 256])
+            total = part if total is None else total + part
+    gp[...] = (total * slope[...]).astype(BF16).astype(F32).reshape(8, 8, 8, 256)
+
     conv.scatter()
+
+    up = AllReduce(place, a_up, fin_up, up_r1, up_s, up_r2, up_r3, up_sems)
+    for parities, (px, py) in enumerate(itertools.product(range(2), repeat=2)):
+        rows = [gp[:, 2 * xc + px, :, 128 * py : 128 * py + 128] for xc in range(4)]
+        grad = jnp.stack(rows, axis=1).reshape(256, 128).astype(BF16)
+        for i, (sx, kx) in enumerate(taps_by_parity[px]):
+            for j, (sy, ky) in enumerate(taps_by_parity[py]):
+                row = 1024 * i + 256 * parities + 128 * j
+                part = nn(uwt[3 * sx + sy], grad)
+                a_up[row : row + 64, :] = part[64:128]
+                a_up[row + 64 : row + 128, :] = jnp.where(low, part[0:64], part[128:192])
+        up.pair(parities, 4)
 
     for x in range(8):
         for zc in range(8):
@@ -420,11 +421,14 @@
             if x in (0, 7):
                 pct[(7 - x) // 7, 0, zc : zc + 1, :] = gp[zc, x, 7:8, 128:256]
                 pct[(7 - x) // 7, 1, zc : zc + 1, :] = gp[zc, x, 0:1, 0:128]
+    up.scatter()
+    conv.exchange()
     p_copies = halo(
         place, pxt, 1, ((8, 0), (1, 9)), None, pys, pyt, pct, pctr, p_sems.at[0], p_sems.at[1]
     )
     up.exchange()
-    conv.exchange()
+    conv.gather()
+    up.gather()
 
     for copy in p_copies.values():
         copy.wait_recv()
@@ -455,16 +459,13 @@
             rows = [jnp.concatenate([pairs[zc], pairs[zc + 1]], axis=1) for zc in range(8)]
             part = nt(jnp.concatenate(rows, axis=0).astype(BF16), w3[4 * kx + ky])
             total = part if total is None else total + part
-        if kx == 1:
-            up.gather()
-    conv.gather()
     total = total.reshape(8, 4, 8, C)
     for zc in range(0, 8, 2):
         co[:, :, 64 * zc : 64 * zc + 128] = jnp.concatenate([total[zc], total[zc + 1]], axis=2).astype(BF16)
     store = pltpu.make_async_copy(co, coarse_out, local_sems.at[5])
     store.start()
-    up.share(out_up, local_sems.at[6])
-    conv.share(out_conv, local_sems.at[7])
+    conv.share(out_conv, local_sems.at[6])
+    up.share(out_up, local_sems.at[7])
     up.finish()
     conv.finish()
     store.wait()
@@ -485,14 +486,17 @@
     stores = []
     for i in range(4):
         loads[i].wait()
-        for q in range(4 * i, 4 * i + 4):
-            first = fin_up[128 * q : 128 * q + 64, :].astype(F32) * factor
-            second = fin_up[128 * q + 64 : 128 * q + 128, :].astype(F32) * factor
+        for s in range(4 * i, 4 * i + 4):
+            half, px, py, j = s // 8, s // 4 % 2, s // 2 % 2, s % 2
+            q = 4 * taps_by_parity[px][half][1] + taps_by_parity[py][j][1]
+            first = fin_up[128 * s : 128 * s + 64, :].astype(F32) * factor
+            second = fin_up[128 * s + 64 : 128 * s + 128, :].astype(F32) * factor
             up[4 * q + 1] = first[:, :C]
             up[4 * q + 2] = first[:, C:]
             up[4 * q + 3] = second[:, :C]
             up[4 * q] = second[:, C:]
-        part = pl.ds(16 * i, 16)
+        kx = taps_by_parity[i % 2][i // 2][1]
+        part = pl.ds(16 * kx, 16)
         stores.append(pltpu.make_async_copy(up.at[part], up_out.at[part], out_sems.at[i]))
         stores[-1].start()
     loads[4].wait()
@@ -515,7 +519,7 @@
     group = sizes[0] // 2 * sizes[1]
     row_group = sizes[2] // 2 * 2
     up_piece, cv_piece = 1024 // group, 512 // group
-    messages = 2 + 2 * (group - 1) + row_group - 1
+    messages = 5 + 2 * (group - 1) + row_group - 1
     vmem = pltpu.VMEM
     dma = pltpu.SemaphoreType.DMA
     anywhere = pl.BlockSpec(memory_space=pl.ANY)

time: 47.2 us -> 45.5 us (0.964)
  Pallas kernels: 46.4 us -> 44.7 us
    pallas_call x1, Pallas kernels: 43.7 us -> 42 us  [local(): pl.pallas_call(functools.partial(main_kernel, sizes), name='halo_compute_...]
where the time goes in v2:
time: 45.5 us; the launch traced here: 45.4 us
  Pallas kernels  44.7 us (98%)
  between operations  0.64 us (1%)
    pallas_call x1, Pallas kernels, local(): pl.pallas_call(functools.partial(main_kernel, sizes), name='halo_compute_...  42 us
    pallas_call x1, Pallas kernels, local(): pl.pallas_call(functools.partial(last_kernel, 1.0 / math.sqrt(every_cell)...  2.74 us

profile of v2, /device:TPU:1, one launch (start us, length us, event | category | flops | bytes accessed | tf_op | source)
XLA Modules:
  0.0 45.4 jit_solution(17264960718568059900)
XLA Ops:
  0.6 42.0 %halo_compute_reduce.1 = (bf16[4,8,512]{2,1,0:T(8,128)(2,1)}, bf16[2048,128]{1,0:T(8,128)(2,1)}, bf16[1024,128]{1,0:T(8,128)(2,1)}) custom-call(bf16[4,8,512]{2,1,0:T(8,128)(2,1)} %u_in.1, bf16[8,16,1024]{2,1,0:T(8,128)(2,1)} %g_in.1, bf16[64,64,64]{2,1,0:T(8,128)(2,1)} %wu_in.1, bf16[27,64,64]{2,1,0:T(8,128)(2,1)} %wc_in.1), custom_call_target="tpu_custom_call" | custom-call | tf_op jit(solution)/shard_map/halo_compute_reduce/pallas_call | solution.py:547
  42.6 2.7 %scale_outputs.1 = (bf16[4,8,512]{2,1,0:T(8,128)(2,1)}, f32[64,64,64]{2,1,0:T(8,128)}, f32[27,64,64]{2,1,0:T(8,128)}) custom-call(bf16[4,8,512]{2,1,0:T(8,128)(2,1)} %get-tuple-element.6.coarse, bf16[2048,128]{1,0:T(8,128)(2,1)} %get-tuple-element.7.in_up, bf16[1024,128]{1,0:T(8,128)(2,1)} %get-tuple-element.8.in_conv), custom_call_target="tpu_custom_call" | custom-call | tf_op jit(solution)/shard_map/scale_outputs/pallas_call | solution.py:562

commit v3 on v2

--- a/solution.py
+++ b/solution.py
@@ -68,11 +68,15 @@
     )
 
 
-def halo(place, xt, edge, faces, extra, ys, yt, ct, ctr, send, recv):
-    copies = {}
+def await_bytes(ref, sem):
+    pltpu.make_async_copy(ref, ref, sem).wait()
+
+
+def halo(place, xt, edge, faces, extra, ys, yt, ct, ctr, sems):
+    copies = []
     planes, lanes = xt.shape[0], xt.shape[2] - 256
     inner = planes - 2 * edge
-    for i, (ox, oy, oz) in enumerate(NEIGHBOURS):
+    for ox, oy, oz in NEIGHBOURS:
         device = place.neighbour((ox, oy, oz))
         zs, zd = {
             0: (pl.ds(0, lanes), pl.ds(128, lanes)),
@@ -96,15 +100,13 @@
             src, dst = ys.at[side, :, zs], yt.at[side, :, zd]
         else:
             src, dst = ct.at[end, side], ctr.at[end, side, 1 - oz]
-        copies[ox, oy, oz] = remote(src, dst, send.at[i], recv.at[i], device)
+        copies.append((src, dst, device))
         if extra is not None and ox != 0 and (oy, oz) == (0, 0):
             source, target = extra
-            copies[ox, None, None] = remote(
-                source.at[end], target.at[end], send.at[26 + end], recv.at[26 + end], device
-            )
-    for copy in copies.values():
-        copy.start()
-    return copies
+            copies.append((source.at[end], target.at[end], device))
+    for src, dst, device in copies:
+        remote(src, dst, sems.at[0], sems.at[1], device).start()
+    return sum(math.prod(src.shape) * jnp.dtype(src.dtype).itemsize for src, _, _ in copies)
 
 
 class AllReduce:
@@ -113,33 +115,28 @@
         self.r1, self.s, self.r2, self.r3, self.sems = r1, s, r2, r3, sems
         self.half = total.shape[0] // 2
         self.piece = self.half // place.group
-        self.used = 0
-        self.flight, self.sent = [], []
+        self.step = -1
+        self.sizes = (r1, r2, r3.at[pl.ds(0, place.row_group - 1)], r2, s)
 
     def send(self, src, dst, device):
-        i = self.used
-        self.used += 1
-        copy = remote(src, dst, self.sems.at[0, i], self.sems.at[1, i], device)
-        copy.start()
-        self.flight.append(copy)
+        remote(src, dst, self.sems.at[0, self.step], self.sems.at[1, self.step], device).start()
 
     def arrive(self):
-        for copy in self.flight:
-            copy.wait_recv()
-        self.sent += self.flight
-        self.flight = []
+        await_bytes(self.sizes[self.step], self.sems.at[1, self.step])
+        self.step += 1
 
     def finish(self):
         self.arrive()
         self.store.wait()
-        for copy in self.sent:
-            copy.wait_send()
+        for step, size in enumerate(self.sizes):
+            await_bytes(size, self.sems.at[0, step])
 
     def mine(self, index, size):
         return pl.ds(pl.multiple_of(index * size, size), size)
 
     def pair(self, part=0, parts=1):
         p = self.place
+        self.step = 0
         size = self.half // parts
         rows = pl.ds(pl.multiple_of((1 - p.core) * self.half + part * size, size), size)
         self.send(self.total.at[rows], self.r1.at[pl.ds(part * size, size)], p.sibling())
@@ -201,7 +198,7 @@
     partners += [place.in_group(*o)[0] for o in place.group_steps()]
     partners += [place.in_row(dy) for dy in range(1, place.row_group)]
     partners += [place.sibling()]
-    for device in partners:
+    for device in partners[:26]:
         pl.semaphore_signal(barrier, inc=1, device_id=device, device_id_type=MESH)
     loads = [
         pltpu.make_async_copy(u_in, ub, local_sems.at[0]),
@@ -212,6 +209,8 @@
     ]
     for load in loads:
         load.start()
+    for device in partners[26:]:
+        pl.semaphore_signal(barrier, inc=1, device_id=device, device_id_type=MESH)
 
     zero_rows = jnp.zeros((4, 1024), F32)
     for side in range(2):
@@ -246,9 +245,7 @@
                 ctf[end, side, 0, 8 + j : 9 + j, :] = ysf[side, 8 + xc : 9 + xc, lane : lane + 128]
             ct[end, side] = ctf[end, side, 0].astype(BF16)
     pl.semaphore_wait(barrier, len(partners))
-    copies = halo(
-        place, xt, 2, ((12, 0), (3, 15)), (uc, uce), ys, yt, ct, ctr, g_sems.at[0], g_sems.at[1]
-    )
+    rim_bytes = halo(place, xt, 2, ((12, 0), (3, 15)), (uc, uce), ys, yt, ct, ctr, g_sems)
 
     loads[3].wait()
     loads[4].wait()
@@ -277,8 +274,7 @@
         cw[128:256, 1024 * dx : 1024 * dx + 256] = jnp.zeros((128, 256), BF16)
         cw[0:128, 1024 * dx + 768 : 1024 * dx + 1024] = jnp.zeros((128, 256), BF16)
 
-    for copy in copies.values():
-        copy.wait_recv()
+    await_bytes(slope.at[pl.ds(0, rim_bytes // 1024)], g_sems.at[1])
     ctf[...] = ctr[...].astype(F32)
     for side in range(2):
         yf[side, 0:16, :] = yt[side].astype(F32)
@@ -330,12 +326,12 @@
     for zc in range(0, 8, 2):
         v = pre[zc : zc + 2].reshape(128, 256)
         square = v * v
-        tangent = jnp.tanh(gelu_coef * (v + gelu_cube * (square * v)))
-        hidden = 0.5 * v * (1.0 + tangent)
+        gate = 0.5 + 0.5 * jnp.tanh(v * (gelu_coef + gelu_coef * gelu_cube * square))
+        hidden = v * gate
         ht[:, 64 * zc : 64 * zc + 128] = hidden.T.astype(BF16)
-        slope[64 * zc : 64 * zc + 128, :] = 0.5 * (1.0 + tangent) + 0.5 * v * (
-            1.0 - tangent * tangent
-        ) * gelu_coef * (1.0 + 3.0 * gelu_cube * square)
+        slope[64 * zc : 64 * zc + 128, :] = gate + hidden * (1.0 - gate) * (
+            2.0 * gelu_coef + 6.0 * gelu_coef * gelu_cube * square
+        )
 
     turn = xt.shape[2] - 64
     for side in range(2):
@@ -400,16 +396,19 @@
     conv.scatter()
 
     up = AllReduce(place, a_up, fin_up, up_r1, up_s, up_r2, up_r3, up_sems)
-    for parities, (px, py) in enumerate(itertools.product(range(2), repeat=2)):
-        rows = [gp[:, 2 * xc + px, :, 128 * py : 128 * py + 128] for xc in range(4)]
-        grad = jnp.stack(rows, axis=1).reshape(256, 128).astype(BF16)
-        for i, (sx, kx) in enumerate(taps_by_parity[px]):
-            for j, (sy, ky) in enumerate(taps_by_parity[py]):
-                row = 1024 * i + 256 * parities + 128 * j
-                part = nn(uwt[3 * sx + sy], grad)
-                a_up[row : row + 64, :] = part[64:128]
-                a_up[row + 64 : row + 128, :] = jnp.where(low, part[0:64], part[128:192])
-        up.pair(parities, 4)
+    for px in range(2):
+        rows = [gp[:, 2 * xc + px, :, :] for xc in range(4)]
+        grad = jnp.stack(rows, axis=1).reshape(256, 256).astype(BF16)
+        product = nn(uwt[3 * px : 3 * px + 6].reshape(1152, 256), grad)
+        for i, (sx, _) in enumerate(taps_by_parity[px]):
+            for py in range(2):
+                for j, (sy, _) in enumerate(taps_by_parity[py]):
+                    row = 1024 * i + 512 * px + 256 * py + 128 * j
+                    first = 192 * (3 * (sx - px) + sy)
+                    part = product[first : first + 192, 128 * py : 128 * py + 128]
+                    a_up[row : row + 64, :] = part[64:128]
+                    a_up[row + 64 : row + 128, :] = jnp.where(low, part[0:64], part[128:192])
+        up.pair(px, 2)
 
     for x in range(8):
         for zc in range(8):
@@ -423,15 +422,12 @@
                 pct[(7 - x) // 7, 1, zc : zc + 1, :] = gp[zc, x, 0:1, 0:128]
     up.scatter()
     conv.exchange()
-    p_copies = halo(
-        place, pxt, 1, ((8, 0), (1, 9)), None, pys, pyt, pct, pctr, p_sems.at[0], p_sems.at[1]
-    )
+    p_bytes = halo(place, pxt, 1, ((8, 0), (1, 9)), None, pys, pyt, pct, pctr, p_sems)
     up.exchange()
     conv.gather()
     up.gather()
 
-    for copy in p_copies.values():
-        copy.wait_recv()
+    await_bytes(slope.at[pl.ds(0, p_bytes // 1024)], p_sems.at[1])
     for side in range(2):
         pyf[side, 0:8, :] = pyt[side]
         for end in range(2):
@@ -469,8 +465,8 @@
     up.finish()
     conv.finish()
     store.wait()
-    for copy in [*copies.values(), *p_copies.values()]:
-        copy.wait_send()
+    await_bytes(slope.at[pl.ds(0, rim_bytes // 1024)], g_sems.at[0])
+    await_bytes(slope.at[pl.ds(0, p_bytes // 1024)], p_sems.at[0])
 
 
 def last_kernel(
@@ -519,7 +515,6 @@
     group = sizes[0] // 2 * sizes[1]
     row_group = sizes[2] // 2 * 2
     up_piece, cv_piece = 1024 // group, 512 // group
-    messages = 5 + 2 * (group - 1) + row_group - 1
     vmem = pltpu.VMEM
     dma = pltpu.SemaphoreType.DMA
     anywhere = pl.BlockSpec(memory_space=pl.ANY)
@@ -542,7 +537,7 @@
         vmem((row_group, up_piece, 128), BF16),
         vmem((512, 128), F32), vmem((512, 128), BF16), vmem((group - 1, cv_piece, 128), BF16),
         vmem((row_group, cv_piece, 128), BF16),
-        dma((8,)), dma((2, 28)), dma((2, 26)), dma((2, messages)), dma((2, messages)),
+        dma((8,)), dma((2,)), dma((2,)), dma((2, 5)), dma((2, 5)),
     ]
     coarse, fin_up, fin_conv = pl.pallas_call(
         functools.partial(main_kernel, sizes),

time: 45.5 us -> 42.5 us (0.934)
  Pallas kernels: 44.7 us -> 41.7 us
    pallas_call x1, Pallas kernels: 42 us -> 39 us  [local(): pl.pallas_call(functools.partial(main_kernel, sizes), name='halo_compute_...]
where the time goes in v3:
time: 42.5 us; the launch traced here: 42.4 us
  Pallas kernels  41.7 us (98%)
  between operations  0.64 us (2%)
    pallas_call x1, Pallas kernels, local(): pl.pallas_call(functools.partial(main_kernel, sizes), name='halo_compute_...  39 us
    pallas_call x1, Pallas kernels, local(): pl.pallas_call(functools.partial(last_kernel, 1.0 / math.sqrt(every_cell)...  2.74 us

profile of v3, /device:TPU:1, one launch (start us, length us, event | category | flops | bytes accessed | tf_op | source)
XLA Modules:
  0.0 42.4 jit_solution(14756826962583753653)
XLA Ops:
  0.6 39.0 %halo_compute_reduce.1 = (bf16[4,8,512]{2,1,0:T(8,128)(2,1)}, bf16[2048,128]{1,0:T(8,128)(2,1)}, bf16[1024,128]{1,0:T(8,128)(2,1)}) custom-call(bf16[4,8,512]{2,1,0:T(8,128)(2,1)} %u_in.1, bf16[8,16,1024]{2,1,0:T(8,128)(2,1)} %g_in.1, bf16[64,64,64]{2,1,0:T(8,128)(2,1)} %wu_in.1, bf16[27,64,64]{2,1,0:T(8,128)(2,1)} %wc_in.1), custom_call_target="tpu_custom_call" | custom-call | tf_op jit(solution)/shard_map/halo_compute_reduce/pallas_call | solution.py:542
  39.6 2.7 %scale_outputs.1 = (bf16[4,8,512]{2,1,0:T(8,128)(2,1)}, f32[64,64,64]{2,1,0:T(8,128)}, f32[27,64,64]{2,1,0:T(8,128)}) custom-call(bf16[4,8,512]{2,1,0:T(8,128)(2,1)} %get-tuple-element.6.coarse, bf16[2048,128]{1,0:T(8,128)(2,1)} %get-tuple-element.7.in_up, bf16[1024,128]{1,0:T(8,128)(2,1)} %get-tuple-element.8.in_conv), custom_call_target="tpu_custom_call" | custom-call | tf_op jit(solution)/shard_map/scale_outputs/pallas_call | solution.py:557

commit v4 on v3

--- a/solution.py
+++ b/solution.py
@@ -110,8 +110,8 @@
 
 
 class AllReduce:
-    def __init__(self, place, total, fin, r1, s, r2, r3, sems):
-        self.place, self.total, self.fin = place, total, fin
+    def __init__(self, place, total, rounded, fin, r1, s, r2, r3, sems):
+        self.place, self.total, self.rounded, self.fin = place, total, rounded, fin
         self.r1, self.s, self.r2, self.r3, self.sems = r1, s, r2, r3, sems
         self.half = total.shape[0] // 2
         self.piece = self.half // place.group
@@ -139,12 +139,12 @@
         self.step = 0
         size = self.half // parts
         rows = pl.ds(pl.multiple_of((1 - p.core) * self.half + part * size, size), size)
-        self.send(self.total.at[rows], self.r1.at[pl.ds(part * size, size)], p.sibling())
+        self.send(self.rounded.at[rows], self.r1.at[pl.ds(part * size, size)], p.sibling())
 
     def scatter(self):
         p = self.place
         self.arrive()
-        self.s[...] = (self.total[self.mine(p.core, self.half), :] + self.r1[...]).astype(BF16)
+        self.s[...] = (self.total[self.mine(p.core, self.half), :] + self.r1[...].astype(F32)).astype(BF16)
         for k, o in enumerate(p.group_steps()):
             device, index = p.in_group(*o)
             self.send(self.s.at[self.mine(index, self.piece)], self.r2.at[k], device)
@@ -156,7 +156,7 @@
         for k in range(p.group - 1):
             total = total + self.r2[k].astype(F32)
         self.r3[p.y] = total.astype(BF16)
-        for dy in range(1, p.row_group):
+        for dy in sorted(range(1, p.row_group), key=lambda d: -min(d, p.row_group - d)):
             self.send(self.r3.at[p.y], self.r3.at[p.y], p.in_row(dy))
 
     def spot(self):
@@ -189,7 +189,7 @@
     ub, wu, wc, ue, ue1, uc, uce, xt, ysf, ys, yt, ct, ctr, ctf, yf, yr, ge, ga, gb,
     wp, cw, w3, uw, uwt, pre, slope, ht, gp,
     pxt, pys, pyt, pct, pctr, pyf, pyr, pe, co, gc,
-    a_up, a_conv, fin_up, fin_conv, up_r1, up_s, up_r2, up_r3, cv_r1, cv_s, cv_r2, cv_r3,
+    a_up, a_conv, b_up, b_conv, fin_up, fin_conv, up_r1, up_s, up_r2, up_r3, cv_r1, cv_s, cv_r2, cv_r3,
     local_sems, g_sems, p_sems, up_sems, cv_sems,
 ):
     place = Place(sizes)
@@ -382,7 +382,8 @@
             joined = gc[8, :, 128:256]
         a_conv[64 * (9 + m) : 64 * (10 + m), :] = joined
     a_conv[896:1024, :] = jnp.zeros((128, 128), F32)
-    conv = AllReduce(place, a_conv, fin_conv, cv_r1, cv_s, cv_r2, cv_r3, cv_sems)
+    b_conv[...] = a_conv[...].astype(BF16)
+    conv = AllReduce(place, a_conv, b_conv, fin_conv, cv_r1, cv_s, cv_r2, cv_r3, cv_sems)
     conv.pair()
 
     total = None
@@ -395,7 +396,7 @@
 
     conv.scatter()
 
-    up = AllReduce(place, a_up, fin_up, up_r1, up_s, up_r2, up_r3, up_sems)
+    up = AllReduce(place, a_up, b_up, fin_up, up_r1, up_s, up_r2, up_r3, up_sems)
     for px in range(2):
         rows = [gp[:, 2 * xc + px, :, :] for xc in range(4)]
         grad = jnp.stack(rows, axis=1).reshape(256, 256).astype(BF16)
@@ -406,8 +407,11 @@
                     row = 1024 * i + 512 * px + 256 * py + 128 * j
                     first = 192 * (3 * (sx - px) + sy)
                     part = product[first : first + 192, 128 * py : 128 * py + 128]
+                    outer = jnp.where(low, part[0:64], part[128:192])
                     a_up[row : row + 64, :] = part[64:128]
-                    a_up[row + 64 : row + 128, :] = jnp.where(low, part[0:64], part[128:192])
+                    a_up[row + 64 : row + 128, :] = outer
+                    b_up[row : row + 64, :] = part[64:128].astype(BF16)
+                    b_up[row + 64 : row + 128, :] = outer.astype(BF16)
         up.pair(px, 2)
 
     for x in range(8):
@@ -533,9 +537,10 @@
         vmem((2, 16, 1152), F32), vmem((9, 10, 2, 24, 128), F32), vmem((4, 8, 512), BF16),
         vmem((9, 64, 256), F32),
         vmem((2048, 128), F32), vmem((1024, 128), F32), vmem((2048, 128), BF16), vmem((1024, 128), BF16),
-        vmem((1024, 128), F32), vmem((1024, 128), BF16), vmem((group - 1, up_piece, 128), BF16),
+        vmem((2048, 128), BF16), vmem((1024, 128), BF16),
+        vmem((1024, 128), BF16), vmem((1024, 128), BF16), vmem((group - 1, up_piece, 128), BF16),
         vmem((row_group, up_piece, 128), BF16),
-        vmem((512, 128), F32), vmem((512, 128), BF16), vmem((group - 1, cv_piece, 128), BF16),
+        vmem((512, 128), BF16), vmem((512, 128), BF16), vmem((group - 1, cv_piece, 128), BF16),
         vmem((row_group, cv_piece, 128), BF16),
         dma((8,)), dma((2,)), dma((2,)), dma((2, 5)), dma((2, 5)),
     ]

time: 42.5 us -> 42.2 us (level)
  no operation moved by 1% of the time
where the time goes in v4:
time: 42.2 us; the launch traced here: 42.1 us
  Pallas kernels  41.4 us (98%)
  between operations  0.64 us (2%)
    pallas_call x1, Pallas kernels, local(): pl.pallas_call(functools.partial(main_kernel, sizes), name='halo_compute_...  38.7 us
    pallas_call x1, Pallas kernels, local(): pl.pallas_call(functools.partial(last_kernel, 1.0 / math.sqrt(every_cell)...  2.74 us

profile of v4, /device:TPU:1, one launch (start us, length us, event | category | flops | bytes accessed | tf_op | source)
XLA Modules:
  0.0 42.1 jit_solution(4895458928699179510)
XLA Ops:
  0.6 38.7 %halo_compute_reduce.1 = (bf16[4,8,512]{2,1,0:T(8,128)(2,1)}, bf16[2048,128]{1,0:T(8,128)(2,1)}, bf16[1024,128]{1,0:T(8,128)(2,1)}) custom-call(bf16[4,8,512]{2,1,0:T(8,128)(2,1)} %u_in.1, bf16[8,16,1024]{2,1,0:T(8,128)(2,1)} %g_in.1, bf16[64,64,64]{2,1,0:T(8,128)(2,1)} %wu_in.1, bf16[27,64,64]{2,1,0:T(8,128)(2,1)} %wc_in.1), custom_call_target="tpu_custom_call" | custom-call | tf_op jit(solution)/shard_map/halo_compute_reduce/pallas_call | solution.py:547
  39.3 2.7 %scale_outputs.1 = (bf16[4,8,512]{2,1,0:T(8,128)(2,1)}, f32[64,64,64]{2,1,0:T(8,128)}, f32[27,64,64]{2,1,0:T(8,128)}) custom-call(bf16[4,8,512]{2,1,0:T(8,128)(2,1)} %get-tuple-element.6.coarse, bf16[2048,128]{1,0:T(8,128)(2,1)} %get-tuple-element.7.in_up, bf16[1024,128]{1,0:T(8,128)(2,1)} %get-tuple-element.8.in_conv), custom_call_target="tpu_custom_call" | custom-call | tf_op jit(solution)/shard_map/scale_outputs/pallas_call | solution.py:562

commit v5 on v4

--- a/solution.py
+++ b/solution.py
@@ -400,12 +400,12 @@
     for px in range(2):
         rows = [gp[:, 2 * xc + px, :, :] for xc in range(4)]
         grad = jnp.stack(rows, axis=1).reshape(256, 256).astype(BF16)
-        product = nn(uwt[3 * px : 3 * px + 6].reshape(1152, 256), grad)
         for i, (sx, _) in enumerate(taps_by_parity[px]):
+            product = nn(uwt[3 * sx : 3 * sx + 3].reshape(576, 256), grad)
             for py in range(2):
                 for j, (sy, _) in enumerate(taps_by_parity[py]):
                     row = 1024 * i + 512 * px + 256 * py + 128 * j
-                    first = 192 * (3 * (sx - px) + sy)
+                    first = 192 * sy
                     part = product[first : first + 192, 128 * py : 128 * py + 128]
                     outer = jnp.where(low, part[0:64], part[128:192])
                     a_up[row : row + 64, :] = part[64:128]

time: 42.2 us -> 42.1 us (level)
  no operation moved by 1% of the time
where the time goes in v5:
time: 42.1 us; the launch traced here: 42 us
  Pallas kernels  41.3 us (98%)
  between operations  0.64 us (2%)
    pallas_call x1, Pallas kernels, local(): pl.pallas_call(functools.partial(main_kernel, sizes), name='halo_compute_...  38.6 us
    pallas_call x1, Pallas kernels, local(): pl.pallas_call(functools.partial(last_kernel, 1.0 / math.sqrt(every_cell)...  2.74 us

profile of v5, /device:TPU:1, one launch (start us, length us, event | category | flops | bytes accessed | tf_op | source)
XLA Modules:
  0.0 42.0 jit_solution(10731263142768225617)
XLA Ops:
  0.6 38.6 %halo_compute_reduce.1 = (bf16[4,8,512]{2,1,0:T(8,128)(2,1)}, bf16[2048,128]{1,0:T(8,128)(2,1)}, bf16[1024,128]{1,0:T(8,128)(2,1)}) custom-call(bf16[4,8,512]{2,1,0:T(8,128)(2,1)} %u_in.1, bf16[8,16,1024]{2,1,0:T(8,128)(2,1)} %g_in.1, bf16[64,64,64]{2,1,0:T(8,128)(2,1)} %wu_in.1, bf16[27,64,64]{2,1,0:T(8,128)(2,1)} %wc_in.1), custom_call_target="tpu_custom_call" | custom-call | tf_op jit(solution)/shard_map/halo_compute_reduce/pallas_call | solution.py:547
  39.2 2.7 %scale_outputs.1 = (bf16[4,8,512]{2,1,0:T(8,128)(2,1)}, f32[64,64,64]{2,1,0:T(8,128)}, f32[27,64,64]{2,1,0:T(8,128)}) custom-call(bf16[4,8,512]{2,1,0:T(8,128)(2,1)} %get-tuple-element.6.coarse, bf16[2048,128]{1,0:T(8,128)(2,1)} %get-tuple-element.7.in_up, bf16[1024,128]{1,0:T(8,128)(2,1)} %get-tuple-element.8.in_conv), custom_call_target="tpu_custom_call" | custom-call | tf_op jit(solution)/shard_map/scale_outputs/pallas_call | solution.py:562
